TPU v7x, 256 devices: a whole 4x4x8 slice. The times are simulated.
256 devices in a mesh: depth: 2 (over y_lo), row: 16 (over z, core), col: 8 (over x, y_hi).
Axes of the slice: x: 4, y: 4 (y_hi: 2, y_lo: 2; y = y_hi * 2 + y_lo), z: 8, core: 2. Of those that a mesh axis runs over, the one named last changes fastest.
Arguments:
- tokens: bfloat16 [1024, 6144], P(('depth', 'col'), 'row'), may hold values from -6 to 6
- w_in: bfloat16 [6144, 24576], P('row', 'col'), may hold values from -0.078125 to 0.078125
- w_out: bfloat16 [24576, 6144], P('col', 'row'), may hold values from -0.0390625 to 0.0390625
- saved: bfloat16 [1024, 24576], P(('depth', 'row'), 'col'), may hold values from -6 to 6
- grad_out: bfloat16 [1024, 6144], P(('depth', 'col'), 'row'), may hold values from -6 to 6
Outputs:
- grad_tokens: bfloat16 [1024, 6144], P(('depth', 'col'), 'row')
- grad_w_in: bfloat16 [6144, 24576], P('row', 'col')
- grad_w_out: bfloat16 [24576, 6144], P('col', 'row')
All inputs are finite; a program needn't handle non-finite values.
Results may differ from a plain program's by a relative error of at most 0.017.
Values may be sent and summed in bfloat16 or wider, within the bound.
A program may use at most 128 MiB of HBM per device.

v0:
```python
import math

import jax
import jax.numpy as jnp
from jax import lax
from jax.sharding import PartitionSpec as P


def normal_cdf(values):
    return 0.5 * (1.0 + jax.scipy.special.erf(values / math.sqrt(2.0)))


def gelu_value(values):
    return values * normal_cdf(values)


def gelu_slope(values):
    normal_pdf = jnp.exp(-0.5 * values * values) / math.sqrt(2.0 * math.pi)
    return normal_cdf(values) + values * normal_pdf


def shards(tokens, w_in, w_out, saved, grad_out):
    contract_last = (((1,), (1,)), ((), ()))
    contract_first = (((0,), (0,)), ((), ()))
    inputs, upstream = (
        lax.all_gather(tokens, "col", axis=0, tiled=True),
        lax.all_gather(grad_out, "col", axis=0, tiled=True),
    )
    row_slice = upstream
    act_grad = lax.psum_scatter(
        lax.dot_general(row_slice, w_out, contract_last, preferred_element_type=jnp.float32),
        "row",
        scatter_dimension=0,
        tiled=True,
    )
    saved_block = saved.astype(jnp.float32)
    hidden_grad = (act_grad * gelu_slope(saved_block)).astype(jnp.bfloat16)
    act_block = gelu_value(saved_block).astype(jnp.bfloat16)
    act_all, hidden_all = (
        lax.all_gather(act_block, "row", axis=0, tiled=True),
        lax.all_gather(hidden_grad, "row", axis=0, tiled=True),
    )
    first_term = lax.dot_general(
        inputs, hidden_all, contract_first, preferred_element_type=jnp.float32
    )
    second_term = lax.dot_general(
        upstream, act_all, contract_first, preferred_element_type=jnp.float32
    )
    summed = lax.psum_scatter(
        jnp.concatenate([first_term, second_term], axis=1).astype(jnp.bfloat16),
        "depth",
        scatter_dimension=0,
        tiled=True,
    )
    combined = lax.all_gather(summed, "depth", axis=0, tiled=True)
    ff_block = w_in.shape[1]
    grad_w_in = combined[:, :ff_block]
    grad_w_out = combined[:, ff_block:].T
    row_slice = hidden_all
    grad_tokens = lax.psum_scatter(
        lax.dot_general(row_slice, w_in, contract_last, preferred_element_type=jnp.float32).astype(
            jnp.bfloat16
        ),
        "col",
        scatter_dimension=0,
        tiled=True,
    )
    return (grad_tokens, grad_w_in, grad_w_out)


def solution(mesh):
    in_specs = (
        P(("depth", "col"), "row"),
        P("row", "col"),
        P("col", "row"),
        P(("depth", "row"), "col"),
        P(("depth", "col"), "row"),
    )
    out_specs = (P(("depth", "col"), "row"), P("row", "col"), P("col", "row"))
    return jax.shard_map(shards, mesh=mesh, in_specs=in_specs, out_specs=out_specs, check_vma=False)
```

profile of v0, /device:TPU:2, one launch (start us, length us, event | category | flops | bytes accessed | tf_op | source)
XLA Modules:
  0.0 436.5 jit_solution(9351496843164270930)
XLA Ops:
  7.2 0.0 reduce-scatter.6.cloned.1.call-start
  7.2 34.7 %all_gather.15 = bf16[512,384]{1,0:T(8,128)(2,1)S(1)} all-gather(bf16[64,384]{1,0:T(8,128)(2,1)} %param.9), channel_id=1, replica_groups=mesh['depth'=2,'row'=16,'col'=8] {'col'}, dimensions={0}, use_global_device_ids=true | all-gather | bytes 442368 | tf_op jit(solution)/shard_map/all_gather | solution.py:27
  42.0 4.5 %fusion.11 = f32[512,3072]{1,0:T(8,128)} fusion(bf16[512,384]{1,0:T(8,128)(2,1)S(1)} %all_gather.15, bf16[3072,384]{1,0:T(8,128)(2,1)S(1)} %copy-done), kind=kOutput, calls=%fused_computation.21 | convolution fusion | flops 1207959552 | bytes 9043968 | tf_op jit(solution)/shard_map/dot_general | solution.py:31
  46.5 0.0 all-gather.6.cloned.1.call-start
  46.5 69.9 %reduce-scatter.6.cloned.1.call-done = f32[32,3072]{1,0:T(8,128)} async-done(((f32[512,3072]{1,0:T(8,128)}), f32[32,3072]{1,0:T(8,128)}) %reduce-scatter.6.cloned.1.call-update) | async-done | bytes 393232 | tf_op jit(solution)/shard_map/reduce_scatter | solution.py:30
  116.4 1.9 fusion.10
  118.4 0.0 all-gather.4.cloned.1.call-start
  118.4 0.7 all-gather.4.cloned.1.call-update
  119.1 0.0 reduce-scatter.10.cloned.1.call-start
  119.2 32.8 %all_gather.17 = bf16[512,384]{1,0:T(8,128)(2,1)S(1)} all-gather(bf16[64,384]{1,0:T(8,128)(2,1)S(1)} %copy-done.3), channel_id=1, replica_groups=mesh['depth'=2,'row'=16,'col'=8] {'col'}, dimensions={0}, use_global_device_ids=true | all-gather | bytes 442368 | tf_op jit(solution)/shard_map/all_gather | solution.py:26
  151.9 6.6 %all-gather.6.cloned.1.call-done = bf16[512,3072]{1,0:T(8,128)(2,1)} async-done(((bf16[32,3072]{1,0:T(8,128)(2,1)}), bf16[512,3072]{1,0:T(8,128)(2,1)}) %all-gather.6.cloned.1.call-update) | async-done | bytes 3145744 | tf_op jit(solution)/shard_map/all_gather | solution.py:40
  158.5 5.1 %fusion.1 = bf16[384,3072]{0,1:T(8,128)(2,1)} fusion(bf16[512,3072]{1,0:T(8,128)(2,1)} %all-gather.6.cloned.1.call-done, bf16[512,384]{1,0:T(8,128)(2,1)S(1)} %all_gather.15), kind=kOutput, calls=%fused_computation.4 | convolution fusion | flops 1209139200 | bytes 5898240 | tf_op jit(solution)/shard_map/dot_general | solution.py:46
  163.6 36.8 %all-gather.4.cloned.1.call-done = bf16[512,3072]{1,0:T(8,128)(2,1)} async-done(((bf16[32,3072]{1,0:T(8,128)(2,1)}), bf16[512,3072]{1,0:T(8,128)(2,1)}) %all-gather.4.cloned.1.call-update) | async-done | bytes 3145744 | tf_op jit(solution)/shard_map/all_gather | solution.py:41
  200.4 3.9 fusion
  204.3 2.7 pad_maximum_fusion
  207.0 6.6 %copy.11 = bf16[384,6144]{1,0:T(8,128)(2,1)} copy(bf16[384,6144]{0,1:T(8,128)(2,1)} %pad_maximum_fusion) | data formatting | bytes 9437184
  213.7 0.0 all-gather.8.cloned.1.call-start
  213.7 63.8 %reduce-scatter.10.cloned.1.call-done = bf16[192,6144]{1,0:T(8,128)(2,1)} async-done(((bf16[384,6144]{1,0:T(8,128)(2,1)}), bf16[192,6144]{1,0:T(8,128)(2,1)}) %reduce-scatter.10.cloned.1.call-update) | async-done | bytes 2359312 | tf_op jit(solution)/shard_map/reduce_scatter | solution.py:49
  277.5 0.0 reduce-scatter.8.cloned.1.call-start
  277.6 5.2 %convolution_convert_fusion.2 = bf16[512,384]{1,0:T(8,128)(2,1)} fusion(bf16[512,3072]{1,0:T(8,128)(2,1)} %all-gather.4.cloned.1.call-done, bf16[384,3072]{1,0:T(8,128)(2,1)} %param.6), kind=kOutput, calls=%fused_computation.6 | convolution fusion | flops 1208156160 | bytes 5898240 | tf_op jit(solution)/shard_map/dot_general | solution.py:61
  282.8 65.3 %all-gather.8.cloned.1.call-done = bf16[384,6144]{1,0:T(8,128)(2,1)} async-done(((bf16[192,6144]{1,0:T(8,128)(2,1)}), bf16[384,6144]{1,0:T(8,128)(2,1)}) %all-gather.8.cloned.1.call-update) | async-done | bytes 4718608 | tf_op jit(solution)/shard_map/all_gather | solution.py:55
  348.1 4.9 %slice_bitcast_fusion = (bf16[3072,384]{0,1:T(8,128)(2,1)}, bf16[384,3072]{1,0:T(8,128)(2,1)}) fusion(bf16[384,6144]{1,0:T(8,128)(2,1)} %all-gather.8.cloned.1.call-done), kind=kLoop, calls=%fused_computation.5 | loop fusion | bytes 9437184 | tf_op jit(solution)/shard_map/transpose | solution.py:58
  352.9 4.3 copy.10
  357.2 72.5 %reduce-scatter.8.cloned.1.call-done = bf16[64,384]{1,0:T(8,128)(2,1)} async-done(((bf16[512,384]{1,0:T(8,128)(2,1)}), bf16[64,384]{1,0:T(8,128)(2,1)}) %reduce-scatter.8.cloned.1.call-update) | async-done | bytes 49168 | tf_op jit(solution)/shard_map/reduce_scatter | solution.py:60
  (13 shorter events, 0.1 us)
Async XLA Ops:
  7.2 34.8 %copy-start = (bf16[3072,384]{1,0:T(8,128)(2,1)S(1)}, bf16[3072,384]{1,0:T(8,128)(2,1)}, u32[]{:S(2)}) copy-start(bf16[3072,384]{1,0:T(8,128)(2,1)} %param.7) | copy-start | bytes 7077892
  7.2 109.2 %reduce-scatter.6.cloned.1.call-start = ((), (), s32[]{:S(2)}) async-start(), calls=%async_computation.3 | async-start | bytes 6684672 | tf_op jit(solution)/shard_map/reduce_scatter | solution.py:30
  46.4 70.0 %copy-start.2 = (bf16[32,3072]{1,0:T(8,128)(2,1)S(1)}, bf16[32,3072]{1,0:T(8,128)(2,1)}, u32[]{:S(2)}) copy-start(bf16[32,3072]{1,0:T(8,128)(2,1)} %param.8) | copy-start | bytes 589828
  46.4 72.7 %copy-start.3 = (bf16[64,384]{1,0:T(8,128)(2,1)S(1)}, bf16[64,384]{1,0:T(8,128)(2,1)}, u32[]{:S(2)}) copy-start(bf16[64,384]{1,0:T(8,128)(2,1)} %param.5) | copy-start | bytes 147460
  46.5 112.0 %all-gather.6.cloned.1.call-start = ((), (), s32[]{:S(2)}) async-start(), calls=%async_computation.6 | async-start | bytes 3342336 | tf_op jit(solution)/shard_map/all_gather | solution.py:40
  118.4 82.1 %all-gather.4.cloned.1.call-start = ((), (), s32[]{:S(2)}) async-start(), calls=%async_computation.4 | async-start | bytes 3342336 | tf_op jit(solution)/shard_map/all_gather | solution.py:41
  119.1 158.4 %reduce-scatter.10.cloned.1.call-start = ((), (), s32[]{:S(2)}) async-start(), calls=%async_computation.8 | async-start | bytes 7077888 | tf_op jit(solution)/shard_map/reduce_scatter | solution.py:49
  200.4 3.9 copy-start.1
  213.7 134.4 %all-gather.8.cloned.1.call-start = ((), (), s32[]{:S(2)}) async-start(), calls=%async_computation.7 | async-start | bytes 7077888 | tf_op jit(solution)/shard_map/all_gather | solution.py:55
  277.5 152.2 %reduce-scatter.8.cloned.1.call-start = ((), (), s32[]{:S(2)}) async-start(), calls=%async_computation.5 | async-start | bytes 442368 | tf_op jit(solution)/shard_map/reduce_scatter | solution.py:60
Sparse Core Ops, SparseCore 0:
  46.6 69.7 reduce-scatter.5
  118.8 39.6 all-gather.5
  160.9 39.4 all-gather.3
  213.8 63.6 reduce-scatter.9
  279.3 68.7 all-gather.7
  352.9 76.7 reduce-scatter.7
where the time goes:
time: 437 us
  waiting for transfers between devices  316 us (72%)
  blocking collectives  67.5 us (15%)
  matrix products  18.7 us (4%)
  local copies, waits for them, and re-layouts  15.8 us (4%)
  between operations  14.1 us (3%)
  other arithmetic  4.59 us (1%)
    reduce_scatter x1, waiting for transfers between devices, shards(): lax.psum_scatter(lax.dot_general(row_slice, w_in, contract_last, preferre...  72.5 us
    reduce_scatter x1, waiting for transfers between devices, shards(): lax.psum_scatter(lax.dot_general(row_slice, w_out, contract_last, preferr...  69.9 us
    all_gather x1, waiting for transfers between devices, shards(): combined = lax.all_gather(summed, 'depth', axis=0, tiled=True)  65.3 us
    reduce_scatter x1, waiting for transfers between devices, shards(): lax.psum_scatter(jnp.concatenate([first_term, second_term], axis=1).astyp...  63.8 us
    all_gather x1, waiting for transfers between devices, shards(): lax.all_gather(hidden_grad, 'row', axis=0, tiled=True)  36.8 us
    all_gather x1, blocking collectives, shards(): lax.all_gather(grad_out, 'col', axis=0, tiled=True)  34.7 us
    all_gather x1, blocking collectives, shards(): lax.all_gather(tokens, 'col', axis=0, tiled=True)  32.8 us
    unnamed x10, local copies, waits for them, and re-layouts  10.9 us
  transfers between devices with their start and end apart: 6, of which 6 were waited for; matrix products, arithmetic and copies ran while one was open for 4% of the time, Pallas kernels for 0%

commit v1 on v0

v1 whole, which is shorter than its diff:
```python
import functools
import math

import jax
import jax.numpy as jnp
from jax import lax
from jax.experimental import pallas as pl
from jax.experimental.pallas import tpu as pltpu
from jax.sharding import PartitionSpec as P

F32, BF16 = jnp.float32, jnp.bfloat16
MESH = pl.DeviceIdType.MESH

CHUNKS = 6
QUARTER = 768
WIDTH = QUARTER // CHUNKS
HALF = 384
FEATURES = 768
TOKENS = 1024
RS_START = 4
SLOTS = RS_START + 8 + CHUNKS

LAST_LAST = (((1,), (1,)), ((), ()))
PLAIN = (((1,), (0,)), ((), ()))


def dot(a, b, dims):
    return lax.dot_general(a, b, dims, preferred_element_type=F32)


def ds(start, size):
    return pl.ds(pl.multiple_of(start, size), size)


def kernel(
    tokens, w_in, w_out, saved, grad_out,
    grad_tokens, grad_w_in, grad_w_out,
    saved_q, up, inp, inp_t, wo, wi, act_t, hid, slope, part,
    rs_out, rs_in, dwo, dwi, tail, sib_out, sib_in,
    x_out, x_in, fin, y_out, y_in,
    local_sem, start_send, start_recv, up_send, up_recv, inp_send, inp_recv,
    act_send, act_recv, rs_send, rs_recv, hid_send, hid_recv,
    dw_local, dw_send, dw_recv, sib_send, sib_recv, x_send, x_recv, y_send, y_recv,
):
    depth, row, col = lax.axis_index("depth"), lax.axis_index("row"), lax.axis_index("col")
    z, core = lax.div(row, 2), lax.rem(row, 2)
    x, y_hi = lax.div(col, 2), lax.rem(col, 2)
    y = y_hi * 2 + depth
    other = 1 - core
    quarter = depth * 2 + core

    def at_y(v):
        v = lax.rem(v + 4, 4)
        return (lax.rem(v, 2), row, x * 2 + lax.div(v, 2))

    def at_x(v):
        return (depth, row, lax.rem(v + 4, 4) * 2 + y_hi)

    def at_z(v):
        return (depth, lax.rem(v + 8, 8) * 2 + core, col)

    to_z = (at_z(z + 1), at_z(z - 1))
    to_x = (at_x(x + 1), at_x(x - 1))
    to_y = (at_y(y + 1), at_y(y - 1))
    sibling = (depth, z * 2 + other, col)
    partner = (1 - depth, row, col)
    diagonal = (1 - depth, z * 2 + other, col)

    def send(src, dst, send_sem, recv_sem, device):
        return pltpu.make_async_remote_copy(
            src_ref=src, dst_ref=dst, send_sem=send_sem, recv_sem=recv_sem,
            device_id=device, device_id_type=MESH,
        )

    mine = ds(core * HALF, HALF)

    own_rows = ds(x * 256 + y * 64, 64)
    locals_ = [
        pltpu.make_async_copy(saved.at[:, ds(quarter * QUARTER, QUARTER)], saved_q.at[quarter], local_sem.at[0]),
        pltpu.make_async_copy(grad_out, up.at[own_rows, mine], local_sem.at[1]),
        pltpu.make_async_copy(tokens, inp.at[own_rows, mine], local_sem.at[2]),
        pltpu.make_async_copy(w_out.at[ds(quarter * QUARTER, QUARTER), :], wo.at[:, mine], local_sem.at[3]),
        pltpu.make_async_copy(w_in.at[:, ds(quarter * QUARTER, QUARTER)], wi.at[mine, :], local_sem.at[4]),
    ]
    for copy in locals_:
        copy.start()
    barrier = pltpu.get_barrier_semaphore()
    for device in (*to_z, *to_x, *to_y, sibling, diagonal):
        pl.semaphore_signal(barrier, inc=1, device_id=device, device_id_type=MESH)
    pl.semaphore_wait(barrier, 8)

    sib_quarter = depth * 2 + other
    starts = []
    for i, (device, q) in enumerate((
        (sibling, sib_quarter),
        (partner, (1 - depth) * 2 + core),
        (diagonal, (1 - depth) * 2 + other),
    )):
        starts.append(send(
            saved.at[:, ds(q * QUARTER, QUARTER)], saved_q.at[quarter],
            start_send.at[i], start_recv.at[i], device,
        ))
    starts.append(send(
        w_out.at[ds(sib_quarter * QUARTER, QUARTER), :], wo.at[:, mine],
        start_send.at[3], start_recv.at[3], sibling,
    ))
    starts.append(send(
        w_in.at[:, ds(sib_quarter * QUARTER, QUARTER)], wi.at[mine, :],
        start_send.at[4], start_recv.at[4], sibling,
    ))

    def gather(source, buf, send_sem, recv_sem):
        def place(v_x, v_y):
            return lax.rem(v_x + 4, 4) * 256 + lax.rem(v_y + 4, 4) * 64

        def block(i, rows, size, device):
            ref = buf.at[ds(rows, size), mine]
            return send(ref, ref, send_sem.at[i], recv_sem.at[i], device)

        own = buf.at[own_rows, mine]
        y0 = send(source, own, send_sem.at[0], recv_sem.at[0], to_y[0])
        y1 = send(source, own, send_sem.at[1], recv_sem.at[1], to_y[1])
        y2 = block(2, place(x, y - 1), 32, to_y[0])
        y3 = block(3, place(x, y + 1) + 32, 32, to_y[1])
        group = lambda v: lax.rem(v + 4, 4) * 256
        x0 = block(4, group(x), 256, to_x[0])
        x1 = block(5, group(x), 256, to_x[1])
        x2 = block(6, group(x - 1), 128, to_x[0])
        x3 = block(7, group(x + 1) + 128, 128, to_x[1])
        s = [block(8 + i, group(x + o), 256, sibling) for i, o in enumerate((0, -1, 1, 2))]
        return y0, y1, y2, y3, x0, x1, x2, x3, *s

    up_copies = gather(grad_out, up, up_send, up_recv)
    inp_copies = gather(tokens, inp, inp_send, inp_recv)

    for copy in starts[:3]:
        copy.start()
    for copy in up_copies[:2]:
        copy.start()
    for copy in inp_copies[:2]:
        copy.start()
    for copy in starts[3:]:
        copy.start()
    for copy in locals_:
        copy.wait()
    for copy in starts[:3]:
        copy.wait_recv()

    def gather_step(copies, stage):
        y0, y1, y2, y3, x0, x1, x2, x3, s0, s1, s2, s3 = copies
        if stage == 0:
            y0.wait_recv()
            y2.start()
            y1.wait_recv()
            y3.start()
        if stage == 1:
            y2.wait_recv()
            y3.wait_recv()
            x0.start()
            x1.start()
            s0.start()
        if stage == 2:
            x0.wait_recv()
            x2.start()
            s1.start()
            x1.wait_recv()
            x3.start()
            s2.start()
        if stage == 3:
            x2.wait_recv()
            x3.wait_recv()
            s3.start()
        if stage == 4:
            for copy in (s0, s1, s2, s3):
                copy.wait_recv()

    def act_copy(j, s, way):
        token_block = ds(lax.rem(z + (8 - s if way == 0 else s), 8) * 128, 128)
        if s == 3:
            rows = pl.ds(way * (WIDTH // 2), WIDTH // 2)
        else:
            rows = pl.ds(0, WIDTH)
        ref = act_t.at[j, rows, token_block]
        return send(ref, ref, act_send.at[j, s, way], act_recv.at[j, s, way], to_z[way])

    def hid_copy(j, s, way):
        start = lax.rem(z + (8 - s if way == 0 else s), 8) * 128
        if s == 3:
            ref = hid.at[j, ds(start + way * 64, 64), :]
        else:
            ref = hid.at[j, ds(start, 128), :]
        return send(ref, ref, hid_send.at[j, s, way], hid_recv.at[j, s, way], to_z[way])

    def rs_copy(j, s, way):
        rows = pl.ds(way * 64, 64) if s == 0 else pl.ds(0, 128)
        return send(
            rs_out.at[j, s, way, rows, :], rs_in.at[j, s, way, rows, :],
            rs_send.at[j, s, way], rs_recv.at[j, s, way], to_z[way],
        )

    def dw_copies(which, j):
        if which == 0:
            place = grad_w_out.at[ds(quarter * QUARTER + j * WIDTH, WIDTH), :]
            blocks = dwo
        else:
            place = grad_w_in.at[:, ds(quarter * QUARTER + j * WIDTH, WIDTH)]
            blocks = dwi
        here = pltpu.make_async_copy(blocks.at[j, core], place, dw_local.at[which, j])
        there = [
            send(blocks.at[j, half], place, dw_send.at[which, j, i], dw_recv.at[which, j, i], device)
            for i, (device, half) in enumerate(((partner, core), (diagonal, other), (sibling, other)))
        ]
        return here, there

    def slot(t, carry):
        def when(j):
            return pl.when(jnp.logical_and(j >= 0, j < CHUNKS))

        @pl.when(t < CHUNKS)
        def _():
            values = saved_q[:, :, ds(t * WIDTH, WIDTH)].reshape(128, WIDTH).astype(F32)
            cdf = 0.5 * (1.0 + lax.erf(values / math.sqrt(2.0)))
            pdf = jnp.exp(-0.5 * values * values) / math.sqrt(2.0 * math.pi)
            slope[t] = cdf + values * pdf
            act_t[t, :, ds(z * 128, 128)] = (values * cdf).T.astype(BF16)
            for way in range(2):
                act_copy(t, 0, way).start()

        for s in range(1, 4):
            @when(t - s)
            def _():
                for way in range(2):
                    act_copy(t - s, s - 1, way).wait_recv()
                    act_copy(t - s, s, way).start()

        for stage in range(5):
            @pl.when(t == stage)
            def _():
                gather_step(up_copies, stage)

        for stage, at in enumerate((0, 2, 3, 4, 5)):
            @pl.when(t == at)
            def _():
                gather_step(inp_copies, stage)

        @pl.when(t == RS_START)
        def _():
            starts[3].wait_recv()

        first = t - RS_START

        @when(first)
        def _():
            j = first
            part[j] = dot(up[...], wo[ds(j * WIDTH, WIDTH), :], LAST_LAST)
            block = lax.rem(z + 4, 8) * 128
            for way in range(2):
                rows = pl.ds(way * 64, 64)
                rs_out[j, 0, way, rows, :] = part[j, ds(block + way * 64, 64), :].astype(BF16)
                rs_copy(j, 0, way).start()

        for s in range(1, 4):
            @when(first - s)
            def _():
                j = first - s
                for way in range(2):
                    rs_copy(j, s - 1, way).wait_recv()
                    block = lax.rem(z + (4 - s if way == 0 else 4 + s), 8) * 128
                    if s == 1:
                        near, far = pl.ds(way * 64, 64), pl.ds((1 - way) * 64, 64)
                        rs_out[j, s, way, near, :] = (
                            part[j, ds(block + way * 64, 64), :] + rs_in[j, 0, way, near, :].astype(F32)
                        ).astype(BF16)
                        rs_out[j, s, way, far, :] = part[j, ds(block + (1 - way) * 64, 64), :].astype(BF16)
                    else:
                        rs_out[j, s, way] = (
                            part[j, ds(block, 128), :] + rs_in[j, s - 1, way].astype(F32)
                        ).astype(BF16)
                    rs_copy(j, s, way).start()

        second = first - 4

        @when(second)
        def _():
            j = second
            for way in range(2):
                rs_copy(j, 3, way).wait_recv()
            mine_z = ds(z * 128, 128)
            total = part[j, mine_z, :] + rs_in[j, 3, 0].astype(F32) + rs_in[j, 3, 1].astype(F32)
            hid[j, mine_z, :] = (total * slope[j]).astype(BF16)
            for way in range(2):
                hid_copy(j, 0, way).start()

        for s in range(1, 4):
            @when(second - s)
            def _():
                for way in range(2):
                    hid_copy(second - s, s - 1, way).wait_recv()
                    hid_copy(second - s, s, way).start()

        @when(t - 4)
        def _():
            j = t - 4
            for way in range(2):
                act_copy(j, 3, way).wait_recv()
            out = dot(act_t[j], up[...], PLAIN).astype(BF16)
            dwo[j, 0] = out[:, :HALF]
            dwo[j, 1] = out[:, HALF:]
            here, there = dw_copies(0, j)
            for copy in there:
                copy.start()
            here.start()

        @when(t - 6)
        def _():
            j = t - 6
            for i in range(FEATURES // 128 // CHUNKS if CHUNKS < 6 else 1):
                columns = (j * (6 // CHUNKS) + i) * 128
                inp_t[ds(columns, 128), :] = inp[:, ds(columns, 128)].astype(F32).T.astype(BF16)

        @when(second - 4)
        def _():
            j = second - 4
            for way in range(2):
                hid_copy(j, 3, way).wait_recv()
            for half in range(2):
                dwi[j, half] = dot(inp_t[pl.ds(half * HALF, HALF), :], hid[j], PLAIN).astype(BF16)
            here, there = dw_copies(1, j)
            for copy in there:
                copy.start()
            here.start()

        return carry

    lax.fori_loop(0, SLOTS, slot, 0)

    starts[4].wait_recv()
    order = (2, 1, 3, 0)

    def sib_copy(i):
        return send(sib_out.at[i], sib_in.at[i], sib_send.at[i], sib_recv.at[i], sibling)

    def partial(i, carry):
        ahead = jnp.where(i == 0, 2, jnp.where(i == 1, 1, jnp.where(i == 2, 3, 0)))
        rows = ds(lax.rem(x + ahead, 4) * 256, 256)
        for half in range(2):
            features = pl.ds(half * HALF, HALF)
            total = dot(hid[0, rows, :], wi[features, pl.ds(0, WIDTH)], LAST_LAST)
            for j in range(1, CHUNKS):
                total += dot(hid[j, rows, :], wi[features, pl.ds(j * WIDTH, WIDTH)], LAST_LAST)
            tail[i, half] = total
        sib_out[i] = tail[i, other].astype(BF16)
        sib_copy(i).start()
        return carry

    lax.fori_loop(0, 4, partial, 0)

    def chip_sum(i, rows):
        return tail[i, core, rows, :] + sib_in[i, rows, :].astype(F32)

    everything = pl.ds(0, 256)

    def x_copy(s, way):
        rows = pl.ds(way * 128, 128) if s == 0 else everything
        return send(
            x_out.at[s, way, rows, :], x_in.at[s, way, rows, :],
            x_send.at[s, way], x_recv.at[s, way], to_x[way],
        )

    sib_copy(0).wait_recv()
    for way in range(2):
        rows = pl.ds(way * 128, 128)
        x_out[0, way, rows, :] = chip_sum(0, rows).astype(BF16)
        x_copy(0, way).start()
    for way in range(2):
        sib_copy(1 + way).wait_recv()
        near, far = pl.ds(way * 128, 128), pl.ds((1 - way) * 128, 128)
        x_out[1, way, far, :] = chip_sum(1 + way, far).astype(BF16)
        x_copy(0, way).wait_recv()
        x_out[1, way, near, :] = (chip_sum(1 + way, near) + x_in[0, way, near, :].astype(F32)).astype(BF16)
        x_copy(1, way).start()
    sib_copy(3).wait_recv()
    fin[...] = chip_sum(3, everything)
    for way in range(2):
        x_copy(1, way).wait_recv()
        fin[...] += x_in[1, way].astype(F32)

    def y_copy(s, way):
        rows = pl.ds(way * 32, 32) if s == 0 else pl.ds(0, 64)
        return send(
            y_out.at[s, way, rows, :], y_in.at[s, way, rows, :],
            y_send.at[s, way], y_recv.at[s, way], to_y[way],
        )

    for way in range(2):
        rows = pl.ds(way * 32, 32)
        y_out[0, way, rows, :] = fin[ds(lax.rem(y + 2, 4) * 64 + way * 32, 32), :].astype(BF16)
        y_copy(0, way).start()
    for way in range(2):
        block = lax.rem(y + (1 if way == 0 else 3), 4) * 64
        near, far = pl.ds(way * 32, 32), pl.ds((1 - way) * 32, 32)
        y_copy(0, way).wait_recv()
        y_out[1, way, far, :] = fin[ds(block + (1 - way) * 32, 32), :].astype(BF16)
        y_out[1, way, near, :] = (
            fin[ds(block + way * 32, 32), :] + y_in[0, way, near, :].astype(F32)
        ).astype(BF16)
        y_copy(1, way).start()
    total = fin[ds(y * 64, 64), :]
    for way in range(2):
        y_copy(1, way).wait_recv()
        total += y_in[1, way].astype(F32)
    grad_tokens[...] = total.astype(BF16)

    for copy in (*starts, *up_copies, *inp_copies):
        copy.wait_send()
    for i in range(4):
        sib_copy(i).wait_send()
    for s in range(2):
        for way in range(2):
            x_copy(s, way).wait_send()
            y_copy(s, way).wait_send()

    def drain(j, carry):
        for s in range(4):
            for way in range(2):
                act_copy(j, s, way).wait_send()
                rs_copy(j, s, way).wait_send()
                hid_copy(j, s, way).wait_send()
        for which in range(2):
            here, there = dw_copies(which, j)
            here.wait()
            for copy in there:
                copy.wait()
        return carry

    lax.fori_loop(0, CHUNKS, drain, 0)


def shards(tokens, w_in, w_out, saved, grad_out):
    any_space = pl.BlockSpec(memory_space=pl.ANY)
    vmem = pl.BlockSpec(memory_space=pltpu.VMEM)
    dma = pltpu.SemaphoreType.DMA
    return pl.pallas_call(
        kernel,
        out_shape=(
            jax.ShapeDtypeStruct(tokens.shape, BF16),
            jax.ShapeDtypeStruct(w_in.shape, BF16),
            jax.ShapeDtypeStruct(w_out.shape, BF16),
        ),
        in_specs=[any_space] * 5,
        out_specs=(vmem, any_space, any_space),
        scratch_shapes=[
            pltpu.VMEM((4, 32, QUARTER), BF16),
            pltpu.VMEM((TOKENS, FEATURES), BF16),
            pltpu.VMEM((TOKENS, FEATURES), BF16),
            pltpu.VMEM((FEATURES, TOKENS), BF16),
            pltpu.VMEM((QUARTER, FEATURES), BF16),
            pltpu.VMEM((FEATURES, QUARTER), BF16),
            pltpu.VMEM((CHUNKS, WIDTH, TOKENS), BF16),
            pltpu.VMEM((CHUNKS, TOKENS, WIDTH), BF16),
            pltpu.VMEM((CHUNKS, 128, WIDTH), F32),
            pltpu.VMEM((CHUNKS, TOKENS, WIDTH), F32),
            pltpu.VMEM((CHUNKS, 4, 2, 128, WIDTH), BF16),
            pltpu.VMEM((CHUNKS, 4, 2, 128, WIDTH), BF16),
            pltpu.VMEM((CHUNKS, 2, WIDTH, HALF), BF16),
            pltpu.VMEM((CHUNKS, 2, HALF, WIDTH), BF16),
            pltpu.VMEM((4, 2, 256, HALF), F32),
            pltpu.VMEM((4, 256, HALF), BF16),
            pltpu.VMEM((4, 256, HALF), BF16),
            pltpu.VMEM((2, 2, 256, HALF), BF16),
            pltpu.VMEM((2, 2, 256, HALF), BF16),
            pltpu.VMEM((256, HALF), F32),
            pltpu.VMEM((2, 2, 64, HALF), BF16),
            pltpu.VMEM((2, 2, 64, HALF), BF16),
            dma((5,)),
            dma((5,)), dma((5,)),
            dma((12,)), dma((12,)),
            dma((12,)), dma((12,)),
            dma((CHUNKS, 4, 2)), dma((CHUNKS, 4, 2)),
            dma((CHUNKS, 4, 2)), dma((CHUNKS, 4, 2)),
            dma((CHUNKS, 4, 2)), dma((CHUNKS, 4, 2)),
            dma((2, CHUNKS)), dma((2, CHUNKS, 3)), dma((2, CHUNKS, 3)),
            dma((4,)), dma((4,)),
            dma((2, 2)), dma((2, 2)),
            dma((2, 2)), dma((2, 2)),
        ],
        compiler_params=pltpu.CompilerParams(
            collective_id=0, has_side_effects=True, vmem_limit_bytes=48 * 2**20
        ),
        name="mlp_backward",
    )(tokens, w_in, w_out, saved, grad_out)


def solution(mesh):
    in_specs = (
        P(("depth", "col"), "row"),
        P("row", "col"),
        P("col", "row"),
        P(("depth", "row"), "col"),
        P(("depth", "col"), "row"),
    )
    out_specs = (P(("depth", "col"), "row"), P("row", "col"), P("col", "row"))
    return jax.shard_map(shards, mesh=mesh, in_specs=in_specs, out_specs=out_specs, check_vma=False)
```

time: 437 us -> 112 us (0.26)
  waiting for transfers between devices: 316 us -> 0 us
  Pallas kernels: 0 us -> 105 us
  blocking collectives: 67.5 us -> 0 us
  matrix products: 18.7 us -> 0 us
  between operations: 14.1 us -> 0.65 us
  local copies, waits for them, and re-layouts: 15.8 us -> 5.95 us
  other arithmetic: 4.59 us -> 0 us
    reduce_scatter x3 -> x0, waiting for transfers between devices: 206 us -> none  [the longest x1 72.5 us: shards(): lax.psum_scatter(lax.dot_general(row_slice, w_in, contract_last, preferre...]
    all_gather x3 -> x0, waiting for transfers between devices: 109 us -> none  [the longest x1 65.3 us: shards(): combined = lax.all_gather(summed, 'depth', axis=0, tiled=True)]
    pallas_call x0 -> x1, Pallas kernels: none -> 105 us  [shards(): pl.pallas_call(kernel, out_shape=(jax.ShapeDtypeStruct(tokens.shape, BF16...]
    all_gather x2 -> x0, blocking collectives: 67.5 us -> none  [the longest x1 34.7 us: shards(): lax.all_gather(grad_out, 'col', axis=0, tiled=True)]
    dot_general x4 -> x0, matrix products: 18.7 us -> none  [the longest x1 5.16 us: shards(): lax.dot_general(row_slice, w_in, contract_last, preferred_element_type=jn...]
    unnamed x10 -> x9, local copies, waits for them, and re-layouts: 10.9 us -> 5.95 us
    transpose x1 -> x0, local copies, waits for them, and re-layouts: 4.88 us -> none  [shards(): grad_w_out = combined[:, ff_block:].T]
  transfers between devices with their start and end apart: 6 -> 0, of which waited for: 6 -> 0; matrix products, arithmetic and copies ran while one was open for 4% -> 0% of each run, Pallas kernels for 0% -> 0%
where the time goes in v1:
time: 112 us; the launch traced here: 111 us
  Pallas kernels  105 us (94%)
  local copies, waits for them, and re-layouts  5.95 us (5%)
    pallas_call x1, Pallas kernels, shards(): pl.pallas_call(kernel, out_shape=(jax.ShapeDtypeStruct(tokens.shape, BF16...  105 us
    unnamed x9, local copies, waits for them, and re-layouts  5.95 us

profile of v1, /device:TPU:2, one launch (start us, length us, event | category | flops | bytes accessed | tf_op | source)
XLA Modules:
  0.0 111.3 jit_solution(14877205950396658878)
XLA Ops:
  0.6 0.0 copy-start
  0.6 0.9 copy-done
  1.6 0.0 copy-start.1
  1.6 0.8 copy-done.1
  2.4 0.0 copy-start.2
  2.4 0.8 copy-done.2
  3.2 104.7 %mlp_backward.1 = (bf16[64,384]{1,0:T(8,128)(2,1)S(1)}, bf16[384,3072]{1,0:T(8,128)(2,1)S(1)}, bf16[3072,384]{1,0:T(8,128)(2,1)S(1)}) custom-call(bf16[64,384]{1,0:T(8,128)(2,1)S(1)} %copy-done.1, bf16[384,3072]{1,0:T(8,128)(2,1)} %w_in.1, bf16[3072,384]{1,0:T(8,128)(2,1)} %w_out.1, bf16[32,3072]{1,0:T(8,128)(2,1)S(1)} %copy-done, bf16[64,384]{1,0:T(8,128)(2,1)S(1)} %copy-done.2), custom_call_target="tpu_custom_call" | custom-call | tf_op jit(solution)/shard_map/mlp_backward/pallas_call | solution.py:443
  107.8 0.6 copy.11
  108.5 1.4 %copy.12 = bf16[384,3072]{1,0:T(8,128)(2,1)} copy(bf16[384,3072]{1,0:T(8,128)(2,1)S(1)} %get-tuple-element.7) | data formatting | bytes 4718592
  109.9 1.4 %copy.13 = bf16[3072,384]{1,0:T(8,128)(2,1)} copy(bf16[3072,384]{1,0:T(8,128)(2,1)S(1)} %get-tuple-element.8) | data formatting | bytes 4718592
Async XLA Ops:
  0.6 0.9 copy-start
  1.6 0.8 copy-start.1
  2.4 0.8 copy-start.2

commit v2 on v1

--- a/solution.py
+++ b/solution.py
@@ -11,7 +11,7 @@
 F32, BF16 = jnp.float32, jnp.bfloat16
 MESH = pl.DeviceIdType.MESH
 
-CHUNKS = 6
+CHUNKS = 3
 QUARTER = 768
 WIDTH = QUARTER // CHUNKS
 HALF = 384
@@ -19,6 +19,9 @@
 TOKENS = 1024
 RS_START = 4
 SLOTS = RS_START + 8 + CHUNKS
+ACT_AT = (0, 1, 2)
+UP_AT = (0, 1, 2, 3, 3)
+INP_AT = (1, 2, 4, 5, 6, 7)
 
 LAST_LAST = (((1,), (1,)), ((), ()))
 PLAIN = (((1,), (0,)), ((), ()))
@@ -109,36 +112,102 @@
         start_send.at[4], start_recv.at[4], sibling,
     ))
 
-    def gather(source, buf, send_sem, recv_sem):
-        def place(v_x, v_y):
-            return lax.rem(v_x + 4, 4) * 256 + lax.rem(v_y + 4, 4) * 64
-
-        def block(i, rows, size, device):
-            ref = buf.at[ds(rows, size), mine]
-            return send(ref, ref, send_sem.at[i], recv_sem.at[i], device)
-
-        own = buf.at[own_rows, mine]
-        y0 = send(source, own, send_sem.at[0], recv_sem.at[0], to_y[0])
-        y1 = send(source, own, send_sem.at[1], recv_sem.at[1], to_y[1])
-        y2 = block(2, place(x, y - 1), 32, to_y[0])
-        y3 = block(3, place(x, y + 1) + 32, 32, to_y[1])
-        group = lambda v: lax.rem(v + 4, 4) * 256
-        x0 = block(4, group(x), 256, to_x[0])
-        x1 = block(5, group(x), 256, to_x[1])
-        x2 = block(6, group(x - 1), 128, to_x[0])
-        x3 = block(7, group(x + 1) + 128, 128, to_x[1])
-        s = [block(8 + i, group(x + o), 256, sibling) for i, o in enumerate((0, -1, 1, 2))]
-        return y0, y1, y2, y3, x0, x1, x2, x3, *s
-
-    up_copies = gather(grad_out, up, up_send, up_recv)
-    inp_copies = gather(tokens, inp, inp_send, inp_recv)
+    def place(d_x, d_y):
+        return lax.rem(x + d_x + 4, 4) * 256 + lax.rem(y + d_y + 4, 4) * 64
+
+    def up_copy(i, rows, size, device, src=None):
+        ref = up.at[ds(rows, size), mine]
+        return send(ref if src is None else src, ref, up_send.at[i], up_recv.at[i], device)
+
+    up_y = (
+        up_copy(0, place(0, 0), 64, to_y[0], grad_out),
+        up_copy(1, place(0, 0), 64, to_y[1], grad_out),
+        up_copy(2, place(0, -1), 32, to_y[0]),
+        up_copy(3, place(0, 1) + 32, 32, to_y[1]),
+    )
+    steps_y = (0, -1, 1, 2)
+    up_x = [
+        [
+            up_copy(4 + 4 * way + k, place(0, d), 64, to_x[way], grad_out if d == 0 else None)
+            for k, d in enumerate(steps_y)
+        ]
+        for way in range(2)
+    ]
+    up_far = (
+        up_copy(12, place(-1, 0), 64, to_x[0]),
+        up_copy(13, place(-1, -1), 64, to_x[0]),
+        up_copy(14, place(1, 1), 64, to_x[1]),
+        up_copy(15, place(1, 2), 64, to_x[1]),
+    )
+    up_sib = [
+        up_copy(16 + i, lax.rem(x + d + 4, 4) * 256, 256, sibling) for i, d in enumerate((0, -1, 1))
+    ] + [up_copy(19 + k, place(2, d), 64, sibling) for k, d in enumerate(steps_y)]
+    up_copies = (*up_y, *up_x[0], *up_x[1], *up_far, *up_sib)
+
+    def up_step(stage):
+        if stage == 0:
+            up_y[0].wait_recv()
+            up_y[2].start()
+            for way in range(2):
+                up_x[way][1].start()
+            up_y[1].wait_recv()
+            up_y[3].start()
+            for way in range(2):
+                up_x[way][2].start()
+            for way in range(2):
+                up_x[way][0].wait_recv()
+            up_far[0].start()
+        if stage == 1:
+            for i in (2, 3):
+                up_y[i].wait_recv()
+            for way in range(2):
+                up_x[way][3].start()
+            up_sib[0].start()
+            for way in range(2):
+                up_x[way][1].wait_recv()
+                up_x[way][2].wait_recv()
+            up_far[1].start()
+            up_far[2].start()
+        if stage == 2:
+            for way in (1, 0):
+                up_x[way][3].wait_recv()
+                if way == 1:
+                    up_far[3].start()
+            up_sib[1].start()
+            up_sib[2].start()
+            up_far[0].wait_recv()
+            up_sib[3].start()
+        if stage == 3:
+            for k in range(1, 4):
+                up_far[k].wait_recv()
+                up_sib[3 + k].start()
+        if stage == 4:
+            for copy in up_sib:
+                copy.wait_recv()
+
+    def inp_copy(i, rows, size, device, src=None):
+        ref = inp.at[ds(rows, size), mine]
+        return send(ref if src is None else src, ref, inp_send.at[i], inp_recv.at[i], device)
+
+    group = lambda d: lax.rem(x + d + 4, 4) * 256
+    inp_copies = (
+        inp_copy(0, place(0, 0), 64, to_y[0], tokens),
+        inp_copy(1, place(0, 0), 64, to_y[1], tokens),
+        inp_copy(2, place(0, -1), 32, to_y[0]),
+        inp_copy(3, place(0, 1) + 32, 32, to_y[1]),
+        inp_copy(4, group(0), 256, to_x[0]),
+        inp_copy(5, group(0), 256, to_x[1]),
+        inp_copy(6, group(-1), 128, to_x[0]),
+        inp_copy(7, group(1) + 128, 128, to_x[1]),
+        *[inp_copy(8 + i, group(d), 256, sibling) for i, d in enumerate((0, -1, 1, 2))],
+    )
 
     for copy in starts[:3]:
         copy.start()
-    for copy in up_copies[:2]:
+    for copy in up_y[:2]:
         copy.start()
-    for copy in inp_copies[:2]:
-        copy.start()
+    for way in range(2):
+        up_x[way][0].start()
     for copy in starts[3:]:
         copy.start()
     for copy in locals_:
@@ -146,31 +215,34 @@
     for copy in starts[:3]:
         copy.wait_recv()
 
-    def gather_step(copies, stage):
-        y0, y1, y2, y3, x0, x1, x2, x3, s0, s1, s2, s3 = copies
+    def inp_step(stage):
+        y0, y1, y2, y3, x0, x1, x2, x3, s0, s1, s2, s3 = inp_copies
         if stage == 0:
+            y0.start()
+            y1.start()
+        if stage == 1:
             y0.wait_recv()
             y2.start()
             y1.wait_recv()
             y3.start()
-        if stage == 1:
+        if stage == 2:
             y2.wait_recv()
             y3.wait_recv()
             x0.start()
             x1.start()
             s0.start()
-        if stage == 2:
+        if stage == 3:
             x0.wait_recv()
             x2.start()
             s1.start()
             x1.wait_recv()
             x3.start()
             s2.start()
-        if stage == 3:
+        if stage == 4:
             x2.wait_recv()
             x3.wait_recv()
             s3.start()
-        if stage == 4:
+        if stage == 5:
             for copy in (s0, s1, s2, s3):
                 copy.wait_recv()
 
@@ -212,47 +284,45 @@
         ]
         return here, there
 
+    def act_at(u):
+        chunk, valid = 0, u == ACT_AT[0]
+        for j in range(1, CHUNKS):
+            chunk = jnp.where(u == ACT_AT[j], j, chunk)
+            valid = jnp.logical_or(valid, u == ACT_AT[j])
+        return chunk, valid
+
     def slot(t, carry):
         def when(j):
             return pl.when(jnp.logical_and(j >= 0, j < CHUNKS))
 
-        @pl.when(t < CHUNKS)
-        def _():
-            values = saved_q[:, :, ds(t * WIDTH, WIDTH)].reshape(128, WIDTH).astype(F32)
+        first = t - RS_START
+        second = first - 4
+
+        j_act, valid = act_at(t)
+
+        @pl.when(valid)
+        def _():
+            j = j_act
+            values = saved_q[:, :, ds(j * WIDTH, WIDTH)].reshape(128, WIDTH).astype(F32)
             cdf = 0.5 * (1.0 + lax.erf(values / math.sqrt(2.0)))
             pdf = jnp.exp(-0.5 * values * values) / math.sqrt(2.0 * math.pi)
-            slope[t] = cdf + values * pdf
-            act_t[t, :, ds(z * 128, 128)] = (values * cdf).T.astype(BF16)
-            for way in range(2):
-                act_copy(t, 0, way).start()
+            slope[j] = cdf + values * pdf
+            act_t[j, :, ds(z * 128, 128)] = (values * cdf).T.astype(BF16)
+            for way in range(2):
+                act_copy(j, 0, way).start()
 
         for s in range(1, 4):
-            @when(t - s)
+            j_act, valid = act_at(t - s)
+
+            @pl.when(valid)
             def _():
                 for way in range(2):
-                    act_copy(t - s, s - 1, way).wait_recv()
-                    act_copy(t - s, s, way).start()
-
-        for stage in range(5):
-            @pl.when(t == stage)
-            def _():
-                gather_step(up_copies, stage)
-
-        for stage, at in enumerate((0, 2, 3, 4, 5)):
-            @pl.when(t == at)
-            def _():
-                gather_step(inp_copies, stage)
-
-        @pl.when(t == RS_START)
-        def _():
-            starts[3].wait_recv()
-
-        first = t - RS_START
+                    act_copy(j_act, s - 1, way).wait_recv()
+                    act_copy(j_act, s, way).start()
 
         @when(first)
         def _():
             j = first
-            part[j] = dot(up[...], wo[ds(j * WIDTH, WIDTH), :], LAST_LAST)
             block = lax.rem(z + 4, 8) * 128
             for way in range(2):
                 rows = pl.ds(way * 64, 64)
@@ -278,8 +348,6 @@
                         ).astype(BF16)
                     rs_copy(j, s, way).start()
 
-        second = first - 4
-
         @when(second)
         def _():
             j = second
@@ -298,25 +366,33 @@
                     hid_copy(second - s, s - 1, way).wait_recv()
                     hid_copy(second - s, s, way).start()
 
-        @when(t - 4)
-        def _():
-            j = t - 4
+        for stage in range(5):
+            @pl.when(t == UP_AT[stage])
+            def _():
+                up_step(stage)
+
+        @pl.when(t == RS_START - 1)
+        def _():
+            starts[3].wait_recv()
+
+        @when(first + 1)
+        def _():
+            j = first + 1
+            part[j] = dot(up[...], wo[ds(j * WIDTH, WIDTH), :], LAST_LAST)
+
+        j_dw, valid = act_at(t - 4)
+
+        @pl.when(valid)
+        def _():
+            j = j_dw
             for way in range(2):
                 act_copy(j, 3, way).wait_recv()
-            out = dot(act_t[j], up[...], PLAIN).astype(BF16)
-            dwo[j, 0] = out[:, :HALF]
-            dwo[j, 1] = out[:, HALF:]
+            for half in range(2):
+                dwo[j, half] = dot(act_t[j], up[:, pl.ds(half * HALF, HALF)], PLAIN).astype(BF16)
             here, there = dw_copies(0, j)
             for copy in there:
                 copy.start()
             here.start()
-
-        @when(t - 6)
-        def _():
-            j = t - 6
-            for i in range(FEATURES // 128 // CHUNKS if CHUNKS < 6 else 1):
-                columns = (j * (6 // CHUNKS) + i) * 128
-                inp_t[ds(columns, 128), :] = inp[:, ds(columns, 128)].astype(F32).T.astype(BF16)
 
         @when(second - 4)
         def _():
@@ -330,12 +406,23 @@
                 copy.start()
             here.start()
 
+        for stage in range(6):
+            @pl.when(t == INP_AT[stage])
+            def _():
+                inp_step(stage)
+
+        @when(t - INP_AT[5] - 1)
+        def _():
+            j = t - INP_AT[5] - 1
+            for i in range(6 // CHUNKS):
+                columns = (j * (6 // CHUNKS) + i) * 128
+                inp_t[ds(columns, 128), :] = inp[:, ds(columns, 128)].astype(F32).T.astype(BF16)
+
         return carry
 
     lax.fori_loop(0, SLOTS, slot, 0)
 
     starts[4].wait_recv()
-    order = (2, 1, 3, 0)
 
     def sib_copy(i):
         return send(sib_out.at[i], sib_in.at[i], sib_send.at[i], sib_recv.at[i], sibling)
@@ -358,64 +445,74 @@
     def chip_sum(i, rows):
         return tail[i, core, rows, :] + sib_in[i, rows, :].astype(F32)
 
-    everything = pl.ds(0, 256)
+    def ends(s, way, size):
+        return pl.ds((1 - way if s == 1 else way) * size, size)
 
     def x_copy(s, way):
-        rows = pl.ds(way * 128, 128) if s == 0 else everything
+        slot, rows = min(s, 1), ends(s, way, 128)
         return send(
-            x_out.at[s, way, rows, :], x_in.at[s, way, rows, :],
+            x_out.at[slot, way, rows, :], x_in.at[slot, way, rows, :],
             x_send.at[s, way], x_recv.at[s, way], to_x[way],
         )
 
     sib_copy(0).wait_recv()
     for way in range(2):
-        rows = pl.ds(way * 128, 128)
+        rows = ends(0, way, 128)
         x_out[0, way, rows, :] = chip_sum(0, rows).astype(BF16)
         x_copy(0, way).start()
     for way in range(2):
         sib_copy(1 + way).wait_recv()
-        near, far = pl.ds(way * 128, 128), pl.ds((1 - way) * 128, 128)
-        x_out[1, way, far, :] = chip_sum(1 + way, far).astype(BF16)
+        rows = ends(1, way, 128)
+        x_out[1, way, rows, :] = chip_sum(1 + way, rows).astype(BF16)
+        x_copy(1, way).start()
+    for way in range(2):
         x_copy(0, way).wait_recv()
-        x_out[1, way, near, :] = (chip_sum(1 + way, near) + x_in[0, way, near, :].astype(F32)).astype(BF16)
-        x_copy(1, way).start()
+        rows = ends(2, way, 128)
+        x_out[1, way, rows, :] = (chip_sum(1 + way, rows) + x_in[0, way, rows, :].astype(F32)).astype(BF16)
+        x_copy(2, way).start()
     sib_copy(3).wait_recv()
-    fin[...] = chip_sum(3, everything)
-    for way in range(2):
-        x_copy(1, way).wait_recv()
-        fin[...] += x_in[1, way].astype(F32)
+    fin[...] = chip_sum(3, pl.ds(0, 256))
+    for s in (1, 2):
+        for way in range(2):
+            x_copy(s, way).wait_recv()
+            rows = ends(s, way, 128)
+            fin[rows, :] += x_in[1, way, rows, :].astype(F32)
 
     def y_copy(s, way):
-        rows = pl.ds(way * 32, 32) if s == 0 else pl.ds(0, 64)
+        slot, rows = min(s, 1), ends(s, way, 32)
         return send(
-            y_out.at[s, way, rows, :], y_in.at[s, way, rows, :],
+            y_out.at[slot, way, rows, :], y_in.at[slot, way, rows, :],
             y_send.at[s, way], y_recv.at[s, way], to_y[way],
         )
 
+    def fin_rows(ahead, s, way):
+        part_at = 32 * (1 - way if s == 1 else way)
+        return fin[ds(lax.rem(y + ahead, 4) * 64 + part_at, 32), :]
+
     for way in range(2):
-        rows = pl.ds(way * 32, 32)
-        y_out[0, way, rows, :] = fin[ds(lax.rem(y + 2, 4) * 64 + way * 32, 32), :].astype(BF16)
+        y_out[0, way, ends(0, way, 32), :] = fin_rows(2, 0, way).astype(BF16)
         y_copy(0, way).start()
     for way in range(2):
-        block = lax.rem(y + (1 if way == 0 else 3), 4) * 64
-        near, far = pl.ds(way * 32, 32), pl.ds((1 - way) * 32, 32)
+        y_out[1, way, ends(1, way, 32), :] = fin_rows(1 + 2 * way, 1, way).astype(BF16)
+        y_copy(1, way).start()
+    for way in range(2):
         y_copy(0, way).wait_recv()
-        y_out[1, way, far, :] = fin[ds(block + (1 - way) * 32, 32), :].astype(BF16)
-        y_out[1, way, near, :] = (
-            fin[ds(block + way * 32, 32), :] + y_in[0, way, near, :].astype(F32)
+        rows = ends(2, way, 32)
+        y_out[1, way, rows, :] = (
+            fin_rows(1 + 2 * way, 2, way) + y_in[0, way, rows, :].astype(F32)
         ).astype(BF16)
-        y_copy(1, way).start()
-    total = fin[ds(y * 64, 64), :]
-    for way in range(2):
-        y_copy(1, way).wait_recv()
-        total += y_in[1, way].astype(F32)
+        y_copy(2, way).start()
+    for s in (1, 2):
+        for way in range(2):
+            y_copy(s, way).wait_recv()
+    total = fin[ds(y * 64, 64), :] + y_in[1, 0].astype(F32) + y_in[1, 1].astype(F32)
     grad_tokens[...] = total.astype(BF16)
 
     for copy in (*starts, *up_copies, *inp_copies):
         copy.wait_send()
     for i in range(4):
         sib_copy(i).wait_send()
-    for s in range(2):
+    for s in range(3):
         for way in range(2):
             x_copy(s, way).wait_send()
             y_copy(s, way).wait_send()
@@ -474,15 +571,15 @@
             pltpu.VMEM((2, 2, 64, HALF), BF16),
             dma((5,)),
             dma((5,)), dma((5,)),
-            dma((12,)), dma((12,)),
+            dma((23,)), dma((23,)),
             dma((12,)), dma((12,)),
             dma((CHUNKS, 4, 2)), dma((CHUNKS, 4, 2)),
             dma((CHUNKS, 4, 2)), dma((CHUNKS, 4, 2)),
             dma((CHUNKS, 4, 2)), dma((CHUNKS, 4, 2)),
             dma((2, CHUNKS)), dma((2, CHUNKS, 3)), dma((2, CHUNKS, 3)),
             dma((4,)), dma((4,)),
-            dma((2, 2)), dma((2, 2)),
-            dma((2, 2)), dma((2, 2)),
+            dma((3, 2)), dma((3, 2)),
+            dma((3, 2)), dma((3, 2)),
         ],
         compiler_params=pltpu.CompilerParams(
             collective_id=0, has_side_effects=True, vmem_limit_bytes=48 * 2**20

time: 112 us -> 101 us (0.902)
  Pallas kernels: 105 us -> 93.2 us
    pallas_call x1, Pallas kernels: 105 us -> 93.2 us  [shards(): pl.pallas_call(kernel, out_shape=(jax.ShapeDtypeStruct(tokens.shape, BF16...]
where the time goes in v2:
time: 101 us; the launch traced here: 99.8 us
  Pallas kernels  93.2 us (92%)
  local copies, waits for them, and re-layouts  5.95 us (6%)
    pallas_call x1, Pallas kernels, shards(): pl.pallas_call(kernel, out_shape=(jax.ShapeDtypeStruct(tokens.shape, BF16...  93.2 us
    unnamed x9, local copies, waits for them, and re-layouts  5.95 us

profile of v2, /device:TPU:2, one launch (start us, length us, event | category | flops | bytes accessed | tf_op | source)
XLA Modules:
  0.0 99.8 jit_solution(3580845276098275564)
XLA Ops:
  0.6 0.0 copy-start
  0.6 0.9 copy-done
  1.6 0.0 copy-start.1
  1.6 0.8 copy-done.1
  2.4 0.0 copy-start.2
  2.4 0.8 copy-done.2
  3.2 93.2 %mlp_backward.1 = (bf16[64,384]{1,0:T(8,128)(2,1)S(1)}, bf16[384,3072]{1,0:T(8,128)(2,1)S(1)}, bf16[3072,384]{1,0:T(8,128)(2,1)S(1)}) custom-call(bf16[64,384]{1,0:T(8,128)(2,1)S(1)} %copy-done.1, bf16[384,3072]{1,0:T(8,128)(2,1)} %w_in.1, bf16[3072,384]{1,0:T(8,128)(2,1)} %w_out.1, bf16[32,3072]{1,0:T(8,128)(2,1)S(1)} %copy-done, bf16[64,384]{1,0:T(8,128)(2,1)S(1)} %copy-done.2), custom_call_target="tpu_custom_call" | custom-call | tf_op jit(solution)/shard_map/mlp_backward/pallas_call | solution.py:540
  96.3 0.6 copy.11
  97.0 1.4 %copy.12 = bf16[384,3072]{1,0:T(8,128)(2,1)} copy(bf16[384,3072]{1,0:T(8,128)(2,1)S(1)} %get-tuple-element.7) | data formatting | bytes 4718592
  98.4 1.4 %copy.13 = bf16[3072,384]{1,0:T(8,128)(2,1)} copy(bf16[3072,384]{1,0:T(8,128)(2,1)S(1)} %get-tuple-element.8) | data formatting | bytes 4718592
Async XLA Ops:
  0.6 0.9 copy-start
  1.6 0.8 copy-start.1
  2.4 0.8 copy-start.2

commit v3 on v2

--- a/solution.py
+++ b/solution.py
@@ -14,14 +14,11 @@
 CHUNKS = 3
 QUARTER = 768
 WIDTH = QUARTER // CHUNKS
+SHARED = (1, 2)
+HIDDEN = CHUNKS + len(SHARED)
 HALF = 384
 FEATURES = 768
 TOKENS = 1024
-RS_START = 4
-SLOTS = RS_START + 8 + CHUNKS
-ACT_AT = (0, 1, 2)
-UP_AT = (0, 1, 2, 3, 3)
-INP_AT = (1, 2, 4, 5, 6, 7)
 
 LAST_LAST = (((1,), (1,)), ((), ()))
 PLAIN = (((1,), (0,)), ((), ()))
@@ -43,7 +40,7 @@
     x_out, x_in, fin, y_out, y_in,
     local_sem, start_send, start_recv, up_send, up_recv, inp_send, inp_recv,
     act_send, act_recv, rs_send, rs_recv, hid_send, hid_recv,
-    dw_local, dw_send, dw_recv, sib_send, sib_recv, x_send, x_recv, y_send, y_recv,
+    dw_local, dw_send, dw_recv, shared_send, shared_recv, sib_send, sib_recv, x_send, x_recv, y_send, y_recv,
 ):
     depth, row, col = lax.axis_index("depth"), lax.axis_index("row"), lax.axis_index("col")
     z, core = lax.div(row, 2), lax.rem(row, 2)
@@ -93,10 +90,11 @@
     pl.semaphore_wait(barrier, 8)
 
     sib_quarter = depth * 2 + other
+    partner_quarter = (1 - depth) * 2 + core
     starts = []
     for i, (device, q) in enumerate((
         (sibling, sib_quarter),
-        (partner, (1 - depth) * 2 + core),
+        (partner, partner_quarter),
         (diagonal, (1 - depth) * 2 + other),
     )):
         starts.append(send(
@@ -275,152 +273,164 @@
             place = grad_w_out.at[ds(quarter * QUARTER + j * WIDTH, WIDTH), :]
             blocks = dwo
         else:
-            place = grad_w_in.at[:, ds(quarter * QUARTER + j * WIDTH, WIDTH)]
+            of, chunk = (quarter, j) if j < CHUNKS else (partner_quarter, SHARED[j - CHUNKS])
+            place = grad_w_in.at[:, ds(of * QUARTER + chunk * WIDTH, WIDTH)]
             blocks = dwi
         here = pltpu.make_async_copy(blocks.at[j, core], place, dw_local.at[which, j])
+        targets = ((sibling, other), (partner, core), (diagonal, other))
+        if which == 1 and (j >= CHUNKS or j in SHARED):
+            targets = targets[:1]
         there = [
             send(blocks.at[j, half], place, dw_send.at[which, j, i], dw_recv.at[which, j, i], device)
-            for i, (device, half) in enumerate(((partner, core), (diagonal, other), (sibling, other)))
+            for i, (device, half) in enumerate(targets)
         ]
         return here, there
 
-    def act_at(u):
-        chunk, valid = 0, u == ACT_AT[0]
-        for j in range(1, CHUNKS):
-            chunk = jnp.where(u == ACT_AT[j], j, chunk)
-            valid = jnp.logical_or(valid, u == ACT_AT[j])
-        return chunk, valid
-
-    def slot(t, carry):
-        def when(j):
-            return pl.when(jnp.logical_and(j >= 0, j < CHUNKS))
-
-        first = t - RS_START
-        second = first - 4
-
-        j_act, valid = act_at(t)
-
-        @pl.when(valid)
-        def _():
-            j = j_act
-            values = saved_q[:, :, ds(j * WIDTH, WIDTH)].reshape(128, WIDTH).astype(F32)
-            cdf = 0.5 * (1.0 + lax.erf(values / math.sqrt(2.0)))
-            pdf = jnp.exp(-0.5 * values * values) / math.sqrt(2.0 * math.pi)
-            slope[j] = cdf + values * pdf
-            act_t[j, :, ds(z * 128, 128)] = (values * cdf).T.astype(BF16)
-            for way in range(2):
-                act_copy(j, 0, way).start()
-
-        for s in range(1, 4):
-            j_act, valid = act_at(t - s)
-
-            @pl.when(valid)
-            def _():
+    def shared_copy(i):
+        rows = ds(z * 128, 128)
+        return send(
+            hid.at[SHARED[i], rows, :], hid.at[CHUNKS + i, rows, :],
+            shared_send.at[i], shared_recv.at[i], partner,
+        )
+
+    def each(step):
+        def body(j, carry):
+            step(j)
+            return carry
+
+        lax.fori_loop(0, CHUNKS, body, 0)
+
+    def act_first(j):
+        values = saved_q[:, :, ds(j * WIDTH, WIDTH)].reshape(128, WIDTH).astype(F32)
+        cdf = 0.5 * (1.0 + lax.erf(values / math.sqrt(2.0)))
+        pdf = jnp.exp(-0.5 * values * values) / math.sqrt(2.0 * math.pi)
+        slope[j] = cdf + values * pdf
+        act_t[j, :, ds(z * 128, 128)] = (values * cdf).T.astype(BF16)
+        for way in range(2):
+            act_copy(j, 0, way).start()
+
+    def act_next(s, j):
+        for way in range(2):
+            act_copy(j, s - 1, way).wait_recv()
+            act_copy(j, s, way).start()
+
+    def rs_first(j):
+        part[j] = dot(up[...], wo[ds(j * WIDTH, WIDTH), :], LAST_LAST)
+        block = lax.rem(z + 4, 8) * 128
+        for way in range(2):
+            rows = pl.ds(way * 64, 64)
+            rs_out[j, 0, way, rows, :] = part[j, ds(block + way * 64, 64), :].astype(BF16)
+            rs_copy(j, 0, way).start()
+
+    def rs_next(s, j):
+        for way in range(2):
+            rs_copy(j, s - 1, way).wait_recv()
+            block = lax.rem(z + (4 - s if way == 0 else 4 + s), 8) * 128
+            if s == 1:
+                near, far = pl.ds(way * 64, 64), pl.ds((1 - way) * 64, 64)
+                rs_out[j, s, way, near, :] = (
+                    part[j, ds(block + way * 64, 64), :] + rs_in[j, 0, way, near, :].astype(F32)
+                ).astype(BF16)
+                rs_out[j, s, way, far, :] = part[j, ds(block + (1 - way) * 64, 64), :].astype(BF16)
+            else:
+                rs_out[j, s, way] = (
+                    part[j, ds(block, 128), :] + rs_in[j, s - 1, way].astype(F32)
+                ).astype(BF16)
+            rs_copy(j, s, way).start()
+
+    def hid_first(j):
+        for way in range(2):
+            rs_copy(j, 3, way).wait_recv()
+        mine_z = ds(z * 128, 128)
+        total = part[j, mine_z, :] + rs_in[j, 3, 0].astype(F32) + rs_in[j, 3, 1].astype(F32)
+        hid[j, mine_z, :] = (total * slope[j]).astype(BF16)
+        for way in range(2):
+            hid_copy(j, 0, way).start()
+
+    def hid_next(s, j):
+        for way in range(2):
+            hid_copy(j, s - 1, way).wait_recv()
+            hid_copy(j, s, way).start()
+
+    def dw_start(which, j):
+        here, there = dw_copies(which, j)
+        for copy in reversed(there):
+            copy.start()
+        here.start()
+
+    def dwo_step(j):
+        for way in range(2):
+            act_copy(j, 3, way).wait_recv()
+        for half in range(2):
+            dwo[j, half] = dot(act_t[j], up[:, pl.ds(half * HALF, HALF)], PLAIN).astype(BF16)
+        dw_start(0, j)
+
+    def hid_last(j):
+        for way in range(2):
+            hid_copy(j, 3, way).wait_recv()
+
+    def dwi_step(j):
+        for half in range(2):
+            dwi[j, half] = dot(inp_t[pl.ds(half * HALF, HALF), :], hid[j], PLAIN).astype(BF16)
+        dw_start(1, j)
+
+    def turn(first, last):
+        def body(b, carry):
+            columns = ds(b * 128, 128)
+            inp_t[columns, :] = inp[:, columns].astype(F32).T.astype(BF16)
+            return carry
+
+        lax.fori_loop(first, last, body, 0)
+
+    each(act_first)
+    up_step(0)
+    inp_step(0)
+    each(functools.partial(act_next, 1))
+    up_step(1)
+    inp_step(1)
+    each(functools.partial(act_next, 2))
+    up_step(2)
+    inp_step(2)
+    each(functools.partial(act_next, 3))
+    up_step(3)
+    starts[3].wait_recv()
+    up_step(4)
+
+    each(rs_first)
+    dwo_step(0)
+    each(functools.partial(rs_next, 1))
+    inp_step(3)
+    dwo_step(1)
+    each(functools.partial(rs_next, 2))
+    inp_step(4)
+    dwo_step(2)
+    each(functools.partial(rs_next, 3))
+    inp_step(5)
+    turn(0, 6)
+
+    each(hid_first)
+    for i in range(len(SHARED)):
+        shared_copy(i).start()
+    for s in range(1, 4):
+        each(functools.partial(hid_next, s))
+
+    def shared_step(s):
+        for i in range(len(SHARED)):
+            if s == 0:
+                shared_copy(i).wait_recv()
                 for way in range(2):
-                    act_copy(j_act, s - 1, way).wait_recv()
-                    act_copy(j_act, s, way).start()
-
-        @when(first)
-        def _():
-            j = first
-            block = lax.rem(z + 4, 8) * 128
-            for way in range(2):
-                rows = pl.ds(way * 64, 64)
-                rs_out[j, 0, way, rows, :] = part[j, ds(block + way * 64, 64), :].astype(BF16)
-                rs_copy(j, 0, way).start()
-
-        for s in range(1, 4):
-            @when(first - s)
-            def _():
-                j = first - s
-                for way in range(2):
-                    rs_copy(j, s - 1, way).wait_recv()
-                    block = lax.rem(z + (4 - s if way == 0 else 4 + s), 8) * 128
-                    if s == 1:
-                        near, far = pl.ds(way * 64, 64), pl.ds((1 - way) * 64, 64)
-                        rs_out[j, s, way, near, :] = (
-                            part[j, ds(block + way * 64, 64), :] + rs_in[j, 0, way, near, :].astype(F32)
-                        ).astype(BF16)
-                        rs_out[j, s, way, far, :] = part[j, ds(block + (1 - way) * 64, 64), :].astype(BF16)
-                    else:
-                        rs_out[j, s, way] = (
-                            part[j, ds(block, 128), :] + rs_in[j, s - 1, way].astype(F32)
-                        ).astype(BF16)
-                    rs_copy(j, s, way).start()
-
-        @when(second)
-        def _():
-            j = second
-            for way in range(2):
-                rs_copy(j, 3, way).wait_recv()
-            mine_z = ds(z * 128, 128)
-            total = part[j, mine_z, :] + rs_in[j, 3, 0].astype(F32) + rs_in[j, 3, 1].astype(F32)
-            hid[j, mine_z, :] = (total * slope[j]).astype(BF16)
-            for way in range(2):
-                hid_copy(j, 0, way).start()
-
-        for s in range(1, 4):
-            @when(second - s)
-            def _():
-                for way in range(2):
-                    hid_copy(second - s, s - 1, way).wait_recv()
-                    hid_copy(second - s, s, way).start()
-
-        for stage in range(5):
-            @pl.when(t == UP_AT[stage])
-            def _():
-                up_step(stage)
-
-        @pl.when(t == RS_START - 1)
-        def _():
-            starts[3].wait_recv()
-
-        @when(first + 1)
-        def _():
-            j = first + 1
-            part[j] = dot(up[...], wo[ds(j * WIDTH, WIDTH), :], LAST_LAST)
-
-        j_dw, valid = act_at(t - 4)
-
-        @pl.when(valid)
-        def _():
-            j = j_dw
-            for way in range(2):
-                act_copy(j, 3, way).wait_recv()
-            for half in range(2):
-                dwo[j, half] = dot(act_t[j], up[:, pl.ds(half * HALF, HALF)], PLAIN).astype(BF16)
-            here, there = dw_copies(0, j)
-            for copy in there:
-                copy.start()
-            here.start()
-
-        @when(second - 4)
-        def _():
-            j = second - 4
-            for way in range(2):
-                hid_copy(j, 3, way).wait_recv()
-            for half in range(2):
-                dwi[j, half] = dot(inp_t[pl.ds(half * HALF, HALF), :], hid[j], PLAIN).astype(BF16)
-            here, there = dw_copies(1, j)
-            for copy in there:
-                copy.start()
-            here.start()
-
-        for stage in range(6):
-            @pl.when(t == INP_AT[stage])
-            def _():
-                inp_step(stage)
-
-        @when(t - INP_AT[5] - 1)
-        def _():
-            j = t - INP_AT[5] - 1
-            for i in range(6 // CHUNKS):
-                columns = (j * (6 // CHUNKS) + i) * 128
-                inp_t[ds(columns, 128), :] = inp[:, ds(columns, 128)].astype(F32).T.astype(BF16)
-
-        return carry
-
-    lax.fori_loop(0, SLOTS, slot, 0)
+                    hid_copy(CHUNKS + i, 0, way).start()
+            elif s < 4:
+                hid_next(s, CHUNKS + i)
+            else:
+                hid_last(CHUNKS + i)
+                dwi_step(CHUNKS + i)
+
+    shared_step(0)
+    for j in range(CHUNKS):
+        hid_last(j)
+        if j not in SHARED:
+            dwi_step(j)
 
     starts[4].wait_recv()
 
@@ -465,11 +475,17 @@
         rows = ends(1, way, 128)
         x_out[1, way, rows, :] = chip_sum(1 + way, rows).astype(BF16)
         x_copy(1, way).start()
+    shared_step(1)
+    for j in SHARED[:1]:
+        dwi_step(j)
     for way in range(2):
         x_copy(0, way).wait_recv()
         rows = ends(2, way, 128)
         x_out[1, way, rows, :] = (chip_sum(1 + way, rows) + x_in[0, way, rows, :].astype(F32)).astype(BF16)
         x_copy(2, way).start()
+    shared_step(2)
+    for j in SHARED[1:]:
+        dwi_step(j)
     sib_copy(3).wait_recv()
     fin[...] = chip_sum(3, pl.ds(0, 256))
     for s in (1, 2):
@@ -495,6 +511,7 @@
     for way in range(2):
         y_out[1, way, ends(1, way, 32), :] = fin_rows(1 + 2 * way, 1, way).astype(BF16)
         y_copy(1, way).start()
+    shared_step(3)
     for way in range(2):
         y_copy(0, way).wait_recv()
         rows = ends(2, way, 32)
@@ -507,6 +524,7 @@
             y_copy(s, way).wait_recv()
     total = fin[ds(y * 64, 64), :] + y_in[1, 0].astype(F32) + y_in[1, 1].astype(F32)
     grad_tokens[...] = total.astype(BF16)
+    shared_step(4)
 
     for copy in (*starts, *up_copies, *inp_copies):
         copy.wait_send()
@@ -523,14 +541,20 @@
                 act_copy(j, s, way).wait_send()
                 rs_copy(j, s, way).wait_send()
                 hid_copy(j, s, way).wait_send()
-        for which in range(2):
+        return carry
+
+    lax.fori_loop(0, CHUNKS, drain, 0)
+    for i in range(len(SHARED)):
+        shared_copy(i).wait_send()
+        for s in range(4):
+            for way in range(2):
+                hid_copy(CHUNKS + i, s, way).wait_send()
+    for which, count in enumerate((CHUNKS, HIDDEN)):
+        for j in range(count):
             here, there = dw_copies(which, j)
             here.wait()
             for copy in there:
                 copy.wait()
-        return carry
-
-    lax.fori_loop(0, CHUNKS, drain, 0)
 
 
 def shards(tokens, w_in, w_out, saved, grad_out):
@@ -554,13 +578,13 @@
             pltpu.VMEM((QUARTER, FEATURES), BF16),
             pltpu.VMEM((FEATURES, QUARTER), BF16),
             pltpu.VMEM((CHUNKS, WIDTH, TOKENS), BF16),
-            pltpu.VMEM((CHUNKS, TOKENS, WIDTH), BF16),
+            pltpu.VMEM((HIDDEN, TOKENS, WIDTH), BF16),
             pltpu.VMEM((CHUNKS, 128, WIDTH), F32),
             pltpu.VMEM((CHUNKS, TOKENS, WIDTH), F32),
             pltpu.VMEM((CHUNKS, 4, 2, 128, WIDTH), BF16),
             pltpu.VMEM((CHUNKS, 4, 2, 128, WIDTH), BF16),
             pltpu.VMEM((CHUNKS, 2, WIDTH, HALF), BF16),
-            pltpu.VMEM((CHUNKS, 2, HALF, WIDTH), BF16),
+            pltpu.VMEM((HIDDEN, 2, HALF, WIDTH), BF16),
             pltpu.VMEM((4, 2, 256, HALF), F32),
             pltpu.VMEM((4, 256, HALF), BF16),
             pltpu.VMEM((4, 256, HALF), BF16),
@@ -575,8 +599,9 @@
             dma((12,)), dma((12,)),
             dma((CHUNKS, 4, 2)), dma((CHUNKS, 4, 2)),
             dma((CHUNKS, 4, 2)), dma((CHUNKS, 4, 2)),
-            dma((CHUNKS, 4, 2)), dma((CHUNKS, 4, 2)),
-            dma((2, CHUNKS)), dma((2, CHUNKS, 3)), dma((2, CHUNKS, 3)),
+            dma((HIDDEN, 4, 2)), dma((HIDDEN, 4, 2)),
+            dma((2, HIDDEN)), dma((2, HIDDEN, 3)), dma((2, HIDDEN, 3)),
+            dma((len(SHARED),)), dma((len(SHARED),)),
             dma((4,)), dma((4,)),
             dma((3, 2)), dma((3, 2)),
             dma((3, 2)), dma((3, 2)),

time: 101 us -> 95.4 us (0.945)
  Pallas kernels: 93.2 us -> 87 us
    pallas_call x1, Pallas kernels: 93.2 us -> 87 us  [shards(): pl.pallas_call(kernel, out_shape=(jax.ShapeDtypeStruct(tokens.shape, BF16...]
where the time goes in v3:
time: 95.4 us; the launch traced here: 93.6 us
  Pallas kernels  87 us (91%)
  local copies, waits for them, and re-layouts  5.95 us (6%)
    pallas_call x1, Pallas kernels, shards(): pl.pallas_call(kernel, out_shape=(jax.ShapeDtypeStruct(tokens.shape, BF16...  87 us
    unnamed x9, local copies, waits for them, and re-layouts  5.95 us

profile of v3, /device:TPU:2, one launch (start us, length us, event | category | flops | bytes accessed | tf_op | source)
XLA Modules:
  0.0 93.6 jit_solution(6057603857052282418)
XLA Ops:
  0.6 0.0 copy-start
  0.6 0.9 copy-done
  1.6 0.0 copy-start.1
  1.6 0.8 copy-done.1
  2.4 0.0 copy-start.2
  2.4 0.8 copy-done.2
  3.2 87.0 %mlp_backward.1 = (bf16[64,384]{1,0:T(8,128)(2,1)S(1)}, bf16[384,3072]{1,0:T(8,128)(2,1)S(1)}, bf16[3072,384]{1,0:T(8,128)(2,1)S(1)}) custom-call(bf16[64,384]{1,0:T(8,128)(2,1)S(1)} %copy-done.1, bf16[384,3072]{1,0:T(8,128)(2,1)} %w_in.1, bf16[3072,384]{1,0:T(8,128)(2,1)} %w_out.1, bf16[32,3072]{1,0:T(8,128)(2,1)S(1)} %copy-done, bf16[64,384]{1,0:T(8,128)(2,1)S(1)} %copy-done.2), custom_call_target="tpu_custom_call" | custom-call | tf_op jit(solution)/shard_map/mlp_backward/pallas_call | solution.py:564
  90.2 0.6 copy.11
  90.8 1.4 %copy.12 = bf16[384,3072]{1,0:T(8,128)(2,1)} copy(bf16[384,3072]{1,0:T(8,128)(2,1)S(1)} %get-tuple-element.7) | data formatting | bytes 4718592
  92.2 1.4 %copy.13 = bf16[3072,384]{1,0:T(8,128)(2,1)} copy(bf16[3072,384]{1,0:T(8,128)(2,1)S(1)} %get-tuple-element.8) | data formatting | bytes 4718592
Async XLA Ops:
  0.6 0.9 copy-start
  1.6 0.8 copy-start.1
  2.4 0.8 copy-start.2

commit v4 on v3

--- a/solution.py
+++ b/solution.py
@@ -85,9 +85,9 @@
     for copy in locals_:
         copy.start()
     barrier = pltpu.get_barrier_semaphore()
-    for device in (*to_z, *to_x, *to_y, sibling, diagonal):
+    for device in (*to_z, *to_x, *to_y, at_y(y + 2), sibling, diagonal):
         pl.semaphore_signal(barrier, inc=1, device_id=device, device_id_type=MESH)
-    pl.semaphore_wait(barrier, 8)
+    pl.semaphore_wait(barrier, 9)
 
     sib_quarter = depth * 2 + other
     partner_quarter = (1 - depth) * 2 + core
@@ -286,12 +286,15 @@
         ]
         return here, there
 
-    def shared_copy(i):
-        rows = ds(z * 128, 128)
+    def shared_copy(i, ahead, at):
+        rows = ds(lax.rem(z + ahead + 8, 8) * 128, 128)
         return send(
             hid.at[SHARED[i], rows, :], hid.at[CHUNKS + i, rows, :],
-            shared_send.at[i], shared_recv.at[i], partner,
+            shared_send.at[at], shared_recv.at[at], partner,
         )
+
+    again = shared_copy(0, 0, 0)
+    across = [shared_copy(1, ahead, 1 + at) for at, ahead in enumerate((0, -1, 1, -2, 2, -3, 3, 4))]
 
     def each(step):
         def body(j, carry):
@@ -391,8 +394,8 @@
     each(functools.partial(act_next, 2))
     up_step(2)
     inp_step(2)
+    up_step(3)
     each(functools.partial(act_next, 3))
-    up_step(3)
     starts[3].wait_recv()
     up_step(4)
 
@@ -409,28 +412,28 @@
     turn(0, 6)
 
     each(hid_first)
-    for i in range(len(SHARED)):
-        shared_copy(i).start()
+    again.start()
+    across[0].start()
     for s in range(1, 4):
         each(functools.partial(hid_next, s))
+        for copy in across[2 * s - 1 : 2 * s + 1]:
+            copy.start()
 
     def shared_step(s):
-        for i in range(len(SHARED)):
-            if s == 0:
-                shared_copy(i).wait_recv()
-                for way in range(2):
-                    hid_copy(CHUNKS + i, 0, way).start()
-            elif s < 4:
-                hid_next(s, CHUNKS + i)
-            else:
-                hid_last(CHUNKS + i)
-                dwi_step(CHUNKS + i)
+        if s == 0:
+            again.wait_recv()
+            for way in range(2):
+                hid_copy(CHUNKS, 0, way).start()
+        elif s < 4:
+            hid_next(s, CHUNKS)
+        else:
+            hid_last(CHUNKS)
+            dwi_step(CHUNKS)
 
     shared_step(0)
     for j in range(CHUNKS):
         hid_last(j)
-        if j not in SHARED:
-            dwi_step(j)
+    across[7].start()
 
     starts[4].wait_recv()
 
@@ -440,17 +443,14 @@
     def partial(i, carry):
         ahead = jnp.where(i == 0, 2, jnp.where(i == 1, 1, jnp.where(i == 2, 3, 0)))
         rows = ds(lax.rem(x + ahead, 4) * 256, 256)
+        block = jnp.concatenate([hid[j, rows, :] for j in range(CHUNKS)], axis=1)
         for half in range(2):
-            features = pl.ds(half * HALF, HALF)
-            total = dot(hid[0, rows, :], wi[features, pl.ds(0, WIDTH)], LAST_LAST)
-            for j in range(1, CHUNKS):
-                total += dot(hid[j, rows, :], wi[features, pl.ds(j * WIDTH, WIDTH)], LAST_LAST)
-            tail[i, half] = total
+            tail[i, half] = dot(block, wi[pl.ds(half * HALF, HALF), :], LAST_LAST)
         sib_out[i] = tail[i, other].astype(BF16)
         sib_copy(i).start()
         return carry
 
-    lax.fori_loop(0, 4, partial, 0)
+    lax.fori_loop(0, 2, partial, 0)
 
     def chip_sum(i, rows):
         return tail[i, core, rows, :] + sib_in[i, rows, :].astype(F32)
@@ -470,22 +470,23 @@
         rows = ends(0, way, 128)
         x_out[0, way, rows, :] = chip_sum(0, rows).astype(BF16)
         x_copy(0, way).start()
+    shared_step(1)
+    lax.fori_loop(2, 4, partial, 0)
     for way in range(2):
         sib_copy(1 + way).wait_recv()
         rows = ends(1, way, 128)
         x_out[1, way, rows, :] = chip_sum(1 + way, rows).astype(BF16)
         x_copy(1, way).start()
-    shared_step(1)
-    for j in SHARED[:1]:
-        dwi_step(j)
+    dwi_step(0)
+    shared_step(2)
     for way in range(2):
         x_copy(0, way).wait_recv()
         rows = ends(2, way, 128)
         x_out[1, way, rows, :] = (chip_sum(1 + way, rows) + x_in[0, way, rows, :].astype(F32)).astype(BF16)
         x_copy(2, way).start()
-    shared_step(2)
-    for j in SHARED[1:]:
-        dwi_step(j)
+    dwi_step(1)
+    dwi_step(2)
+    shared_step(3)
     sib_copy(3).wait_recv()
     fin[...] = chip_sum(3, pl.ds(0, 256))
     for s in (1, 2):
@@ -494,37 +495,23 @@
             rows = ends(s, way, 128)
             fin[rows, :] += x_in[1, way, rows, :].astype(F32)
 
-    def y_copy(s, way):
-        slot, rows = min(s, 1), ends(s, way, 32)
-        return send(
-            y_out.at[slot, way, rows, :], y_in.at[slot, way, rows, :],
-            y_send.at[s, way], y_recv.at[s, way], to_y[way],
-        )
-
-    def fin_rows(ahead, s, way):
-        part_at = 32 * (1 - way if s == 1 else way)
-        return fin[ds(lax.rem(y + ahead, 4) * 64 + part_at, 32), :]
-
-    for way in range(2):
-        y_out[0, way, ends(0, way, 32), :] = fin_rows(2, 0, way).astype(BF16)
-        y_copy(0, way).start()
-    for way in range(2):
-        y_out[1, way, ends(1, way, 32), :] = fin_rows(1 + 2 * way, 1, way).astype(BF16)
-        y_copy(1, way).start()
-    shared_step(3)
-    for way in range(2):
-        y_copy(0, way).wait_recv()
-        rows = ends(2, way, 32)
-        y_out[1, way, rows, :] = (
-            fin_rows(1 + 2 * way, 2, way) + y_in[0, way, rows, :].astype(F32)
-        ).astype(BF16)
-        y_copy(2, way).start()
-    for s in (1, 2):
-        for way in range(2):
-            y_copy(s, way).wait_recv()
-    total = fin[ds(y * 64, 64), :] + y_in[1, 0].astype(F32) + y_in[1, 1].astype(F32)
+    aheads = (2, 1, 3)
+
+    def y_copy(i):
+        return send(y_out.at[i], y_in.at[i], y_send.at[i], y_recv.at[i], at_y(y + aheads[i]))
+
+    for i, ahead in enumerate(aheads):
+        y_out[i] = fin[ds(lax.rem(y + ahead, 4) * 64, 64), :].astype(BF16)
+        y_copy(i).start()
+    for copy in across:
+        copy.wait_recv()
+    dwi_step(CHUNKS + 1)
+    shared_step(4)
+    total = fin[ds(y * 64, 64), :]
+    for i in range(3):
+        y_copy(i).wait_recv()
+        total += y_in[i].astype(F32)
     grad_tokens[...] = total.astype(BF16)
-    shared_step(4)
 
     for copy in (*starts, *up_copies, *inp_copies):
         copy.wait_send()
@@ -533,7 +520,7 @@
     for s in range(3):
         for way in range(2):
             x_copy(s, way).wait_send()
-            y_copy(s, way).wait_send()
+        y_copy(s).wait_send()
 
     def drain(j, carry):
         for s in range(4):
@@ -544,11 +531,11 @@
         return carry
 
     lax.fori_loop(0, CHUNKS, drain, 0)
-    for i in range(len(SHARED)):
-        shared_copy(i).wait_send()
-        for s in range(4):
-            for way in range(2):
-                hid_copy(CHUNKS + i, s, way).wait_send()
+    for copy in (again, *across):
+        copy.wait_send()
+    for s in range(4):
+        for way in range(2):
+            hid_copy(CHUNKS, s, way).wait_send()
     for which, count in enumerate((CHUNKS, HIDDEN)):
         for j in range(count):
             here, there = dw_copies(which, j)
@@ -591,8 +578,8 @@
             pltpu.VMEM((2, 2, 256, HALF), BF16),
             pltpu.VMEM((2, 2, 256, HALF), BF16),
             pltpu.VMEM((256, HALF), F32),
-            pltpu.VMEM((2, 2, 64, HALF), BF16),
-            pltpu.VMEM((2, 2, 64, HALF), BF16),
+            pltpu.VMEM((3, 64, HALF), BF16),
+            pltpu.VMEM((3, 64, HALF), BF16),
             dma((5,)),
             dma((5,)), dma((5,)),
             dma((23,)), dma((23,)),
@@ -601,10 +588,10 @@
             dma((CHUNKS, 4, 2)), dma((CHUNKS, 4, 2)),
             dma((HIDDEN, 4, 2)), dma((HIDDEN, 4, 2)),
             dma((2, HIDDEN)), dma((2, HIDDEN, 3)), dma((2, HIDDEN, 3)),
-            dma((len(SHARED),)), dma((len(SHARED),)),
+            dma((9,)), dma((9,)),
             dma((4,)), dma((4,)),
             dma((3, 2)), dma((3, 2)),
-            dma((3, 2)), dma((3, 2)),
+            dma((3,)), dma((3,)),
         ],
         compiler_params=pltpu.CompilerParams(
             collective_id=0, has_side_effects=True, vmem_limit_bytes=48 * 2**20

time: 95.4 us -> 91.9 us (0.963); the launches traced: 93.6 us -> 91.3 us
  Pallas kernels: 87 us -> 84.7 us
    pallas_call x1, Pallas kernels: 87 us -> 84.7 us  [shards(): pl.pallas_call(kernel, out_shape=(jax.ShapeDtypeStruct(tokens.shape, BF16...]
where the time goes in v4:
time: 91.9 us; the launch traced here: 91.3 us
  Pallas kernels  84.7 us (92%)
  local copies, waits for them, and re-layouts  5.95 us (6%)
    pallas_call x1, Pallas kernels, shards(): pl.pallas_call(kernel, out_shape=(jax.ShapeDtypeStruct(tokens.shape, BF16...  84.7 us
    unnamed x9, local copies, waits for them, and re-layouts  5.95 us

profile of v4, /device:TPU:2, one launch (start us, length us, event | category | flops | bytes accessed | tf_op | source)
XLA Modules:
  0.0 91.3 jit_solution(13852585848070368022)
XLA Ops:
  0.6 0.0 copy-start
  0.6 0.9 %copy-done = bf16[32,3072]{1,0:T(8,128)(2,1)S(1)} copy-done((bf16[32,3072]{1,0:T(8,128)(2,1)S(1)}, bf16[32,3072]{1,0:T(8,128)(2,1)}, u32[]{:S(2)}) %copy-start) | copy-done | bytes 196632
  1.6 0.0 copy-start.1
  1.6 0.8 copy-done.1
  2.4 0.0 copy-start.2
  2.4 0.8 copy-done.2
  3.2 84.7 %mlp_backward.1 = (bf16[64,384]{1,0:T(8,128)(2,1)S(1)}, bf16[384,3072]{1,0:T(8,128)(2,1)S(1)}, bf16[3072,384]{1,0:T(8,128)(2,1)S(1)}) custom-call(bf16[64,384]{1,0:T(8,128)(2,1)S(1)} %copy-done.1, bf16[384,3072]{1,0:T(8,128)(2,1)} %w_in.1, bf16[3072,384]{1,0:T(8,128)(2,1)} %w_out.1, bf16[32,3072]{1,0:T(8,128)(2,1)S(1)} %copy-done, bf16[64,384]{1,0:T(8,128)(2,1)S(1)} %copy-done.2), custom_call_target="tpu_custom_call" | custom-call | tf_op jit(solution)/shard_map/mlp_backward/pallas_call | solution.py:551
  87.9 0.6 copy.11
  88.5 1.4 %copy.12 = bf16[384,3072]{1,0:T(8,128)(2,1)} copy(bf16[384,3072]{1,0:T(8,128)(2,1)S(1)} %get-tuple-element.7) | data formatting | bytes 4718592
  89.9 1.4 %copy.13 = bf16[3072,384]{1,0:T(8,128)(2,1)} copy(bf16[3072,384]{1,0:T(8,128)(2,1)S(1)} %get-tuple-element.8) | data formatting | bytes 4718592
Async XLA Ops:
  0.6 0.9 %copy-start = (bf16[32,3072]{1,0:T(8,128)(2,1)S(1)}, bf16[32,3072]{1,0:T(8,128)(2,1)}, u32[]{:S(2)}) copy-start(bf16[32,3072]{1,0:T(8,128)(2,1)} %saved.1) | copy-start | bytes 589828
  1.6 0.8 copy-start.1
  2.4 0.8 copy-start.2

commit v5 on v4

--- a/solution.py
+++ b/solution.py
@@ -206,9 +206,7 @@
         copy.start()
     for way in range(2):
         up_x[way][0].start()
-    for copy in starts[3:]:
-        copy.start()
-    for copy in locals_:
+    for copy in locals_[:2]:
         copy.wait()
     for copy in starts[:3]:
         copy.wait_recv()
@@ -386,32 +384,36 @@
         lax.fori_loop(first, last, body, 0)
 
     each(act_first)
+    for copy in starts[3:]:
+        copy.start()
     up_step(0)
-    inp_step(0)
     each(functools.partial(act_next, 1))
     up_step(1)
-    inp_step(1)
+    inp_step(0)
     each(functools.partial(act_next, 2))
     up_step(2)
-    inp_step(2)
+    inp_step(1)
     up_step(3)
     each(functools.partial(act_next, 3))
     starts[3].wait_recv()
+    for copy in locals_[2:]:
+        copy.wait()
     up_step(4)
 
     each(rs_first)
     dwo_step(0)
     each(functools.partial(rs_next, 1))
-    inp_step(3)
+    inp_step(2)
     dwo_step(1)
     each(functools.partial(rs_next, 2))
-    inp_step(4)
+    inp_step(3)
     dwo_step(2)
     each(functools.partial(rs_next, 3))
+    inp_step(4)
+
+    each(hid_first)
     inp_step(5)
     turn(0, 6)
-
-    each(hid_first)
     again.start()
     across[0].start()
     for s in range(1, 4):

time: 91.9 us -> 91.3 us (level)
  no operation moved by 1% of the time
where the time goes in v5:
time: 91.3 us; the launch traced here: 90.7 us
  Pallas kernels  84.1 us (92%)
  local copies, waits for them, and re-layouts  5.95 us (7%)
    pallas_call x1, Pallas kernels, shards(): pl.pallas_call(kernel, out_shape=(jax.ShapeDtypeStruct(tokens.shape, BF16...  84.1 us
    unnamed x9, local copies, waits for them, and re-layouts  5.95 us

profile of v5, /device:TPU:2, one launch (start us, length us, event | category | flops | bytes accessed | tf_op | source)
XLA Modules:
  0.0 90.7 jit_solution(14952652499285756319)
XLA Ops:
  0.6 0.0 copy-start
  0.6 0.9 %copy-done = bf16[32,3072]{1,0:T(8,128)(2,1)S(1)} copy-done((bf16[32,3072]{1,0:T(8,128)(2,1)S(1)}, bf16[32,3072]{1,0:T(8,128)(2,1)}, u32[]{:S(2)}) %copy-start) | copy-done | bytes 196632
  1.6 0.0 copy-start.1
  1.6 0.8 copy-done.1
  2.4 0.0 copy-start.2
  2.4 0.8 copy-done.2
  3.2 84.1 %mlp_backward.1 = (bf16[64,384]{1,0:T(8,128)(2,1)S(1)}, bf16[384,3072]{1,0:T(8,128)(2,1)S(1)}, bf16[3072,384]{1,0:T(8,128)(2,1)S(1)}) custom-call(bf16[64,384]{1,0:T(8,128)(2,1)S(1)} %copy-done.1, bf16[384,3072]{1,0:T(8,128)(2,1)} %w_in.1, bf16[3072,384]{1,0:T(8,128)(2,1)} %w_out.1, bf16[32,3072]{1,0:T(8,128)(2,1)S(1)} %copy-done, bf16[64,384]{1,0:T(8,128)(2,1)S(1)} %copy-done.2), custom_call_target="tpu_custom_call" | custom-call | tf_op jit(solution)/shard_map/mlp_backward/pallas_call | solution.py:553
  87.3 0.6 copy.11
  87.9 1.4 %copy.12 = bf16[384,3072]{1,0:T(8,128)(2,1)} copy(bf16[384,3072]{1,0:T(8,128)(2,1)S(1)} %get-tuple-element.7) | data formatting | bytes 4718592
  89.3 1.4 %copy.13 = bf16[3072,384]{1,0:T(8,128)(2,1)} copy(bf16[3072,384]{1,0:T(8,128)(2,1)S(1)} %get-tuple-element.8) | data formatting | bytes 4718592
Async XLA Ops:
  0.6 0.9 %copy-start = (bf16[32,3072]{1,0:T(8,128)(2,1)S(1)}, bf16[32,3072]{1,0:T(8,128)(2,1)}, u32[]{:S(2)}) copy-start(bf16[32,3072]{1,0:T(8,128)(2,1)} %saved.1) | copy-start | bytes 589828
  1.6 0.8 copy-start.1
  2.4 0.8 copy-start.2
